TPU v7x, 256 devices: a whole 4x4x8 slice. The times are simulated.
256 devices in a mesh: patch: 32 (over z, y_lo, core), uly: 8 (over y_hi, x).
Axes of the slice: x: 4, y: 4 (y_hi: 2, y_lo: 2; y = y_hi * 2 + y_lo), z: 8, core: 2. Of those that a mesh axis runs over, the one named last changes fastest.
Arguments:
- qkv: bfloat16 [3, 10240, 2048], P(None, ('patch', 'uly')), may hold values from -16 to 16
- stale_kv: bfloat16 [2, 10240, 2048], P(None, 'patch', 'uly'), may hold values from -16 to 16
- out_weight: bfloat16 [2048, 3072], P('uly'), may hold values from -0.125 to 0.125
Outputs:
- mixed: bfloat16 [10240, 3072], P(('patch', 'uly'))
- fresh_kv: bfloat16 [2, 10240, 2048], P(None, 'patch', 'uly')
All inputs are finite; a program needn't handle non-finite values.
Results may differ from a plain program's by a relative error of at most 0.018.
Values may be sent and summed in bfloat16 or wider, within the bound.
A program may use at most 128 MiB of HBM per device.

v0:
```python
import jax
import jax.numpy as jnp
from jax import lax
from jax.sharding import PartitionSpec as P

HEAD_DIM = 128


def block_length(row_count):
    for candidate in range(min(row_count, 2048), 0, -1):
        if row_count % candidate == 0:
            return candidate
    return 1


def score_block(queries, key_block):
    scores = jnp.einsum("qhd,khd->qhk", queries, key_block, preferred_element_type=jnp.float32)
    return scores * HEAD_DIM ** (-0.5)


def on_device(qkv, stale_kv, out_weight):
    exchanged = lax.all_to_all(qkv, "uly", split_axis=2, concat_axis=1, tiled=True)
    group_size = exchanged.shape[1]
    row_width = exchanged.shape[2]
    head_count = row_width // HEAD_DIM
    queries = exchanged[0].reshape(group_size, head_count, HEAD_DIM)
    fresh_keys = exchanged[1].reshape(group_size, head_count, HEAD_DIM)
    fresh_values = exchanged[2].reshape(group_size, head_count, HEAD_DIM)
    scores = score_block(queries, fresh_keys)
    row_max = jnp.max(scores, axis=2)
    weights = jnp.exp(scores - row_max[:, :, None])
    row_total = jnp.sum(weights, axis=2)
    summed = jnp.einsum(
        "qhk,khd->qhd",
        weights.astype(jnp.bfloat16),
        fresh_values,
        preferred_element_type=jnp.float32,
    )
    own_group = lax.axis_index("patch")
    first_row = jnp.int32(0)
    key_rows = lax.all_gather(stale_kv[0], "patch", axis=0, tiled=True)
    value_rows = lax.all_gather(stale_kv[1], "patch", axis=0, tiled=True)
    row_count = key_rows.shape[0]
    block_size = block_length(row_count)
    block_count = row_count // block_size

    def advance(block_index, current):
        old_max, old_total, old_summed = current
        block_offset = block_index * block_size
        key_block = lax.dynamic_slice_in_dim(key_rows, block_offset, block_size, 0)
        value_block = lax.dynamic_slice_in_dim(value_rows, block_offset, block_size, 0)
        key_block = key_block.reshape(block_size, head_count, HEAD_DIM)
        value_block = value_block.reshape(block_size, head_count, HEAD_DIM)
        block_scores = score_block(queries, key_block)
        positions = first_row + block_offset + jnp.arange(block_size, dtype=jnp.int32)
        foreign = positions // group_size != own_group
        block_scores = jnp.where(foreign[None, None, :], block_scores, -jnp.inf)
        new_max = jnp.maximum(old_max, jnp.max(block_scores, axis=2))
        factor = jnp.exp(old_max - new_max)
        block_weights = jnp.exp(block_scores - new_max[:, :, None])
        new_total = old_total * factor + jnp.sum(block_weights, axis=2)
        new_summed = old_summed * factor[:, :, None] + jnp.einsum(
            "qhk,khd->qhd",
            block_weights.astype(jnp.bfloat16),
            value_block,
            preferred_element_type=jnp.float32,
        )
        return (new_max, new_total, new_summed)

    row_max, row_total, summed = lax.fori_loop(
        0, block_count, advance, (row_max, row_total, summed)
    )
    attended = (summed / row_total[:, :, None]).astype(jnp.bfloat16).reshape(group_size, row_width)
    mixed = lax.psum_scatter(
        jnp.dot(attended, out_weight, preferred_element_type=jnp.float32).astype(jnp.bfloat16),
        "uly",
        scatter_dimension=0,
        tiled=True,
    )
    return (mixed, exchanged[1:3])


def solution(mesh):
    placed = (P(None, ("patch", "uly"), None), P(None, "patch", "uly"), P("uly", None))
    return jax.shard_map(
        on_device,
        mesh=mesh,
        in_specs=placed,
        out_specs=(P(("patch", "uly"), None), P(None, "patch", "uly")),
        check_vma=False,
    )
```

profile of v0, /device:TPU:1, one launch (start us, length us, event | category | flops | bytes accessed | tf_op | source)
XLA Modules:
  0.0 302.2 jit_solution(9395940351010558202)
XLA Ops:
  7.2 0.0 copy-start
  7.2 0.0 all-gather.7.cloned.1.call-start
  7.2 1.8 fusion.28
  9.1 0.0 all-gather.7.cloned.1.call-update
  9.1 0.0 all-gather.5.cloned.1.call-start
  9.1 0.7 all-gather.5.cloned.1.call-update
  9.9 4.0 %copy.20 = bf16[3,40,2048]{1,0,2:T(4,128)(2,1)} copy(bf16[3,40,2048]{2,1,0:T(8,128)(2,1)} %param.5) | data formatting | bytes 983040 | tf_op args[0]
  13.8 4.7 %reshape.54 = bf16[8,2,15360]{2,1,0:T(2,128)(2,1)} reshape(bf16[2048,3,40]{2,1,0:T(4,128)(2,1)} %bitcast.69) | data formatting | bytes 983040
  18.6 7.5 %all-to-all-start = ((bf16[8,2,15360]{2,1,0:T(2,128)(2,1)}), bf16[8,2,15360]{2,1,0:T(2,128)(2,1)S(1)}, u32[]{:S(2)}, u32[]{:S(2)}) async-start(bf16[8,2,15360]{2,1,0:T(2,128)(2,1)} %reshape.54), calls=%async_computation | async-start | bytes 983040 | tf_op jit(solution)/shard_map/all_to_all | solution.py:22
  26.1 0.0 reduce-scatter.2.cloned.1.call-start
  26.1 11.3 %all-to-all-done = bf16[8,2,15360]{2,1,0:T(2,128)(2,1)S(1)} async-done(((bf16[8,2,15360]{2,1,0:T(2,128)(2,1)}), bf16[8,2,15360]{2,1,0:T(2,128)(2,1)S(1)}, u32[]{:S(2)}, u32[]{:S(2)}) %all-to-all-start) | async-done | bytes 491552 | tf_op jit(solution)/shard_map/all_to_all | solution.py:22
  37.4 3.6 %reshape.55 = bf16[2048,3,40]{2,1,0:T(4,128)(2,1)} reshape(bf16[8,2,15360]{2,1,0:T(2,128)(2,1)S(1)} %all-to-all-done) | data formatting | bytes 983040
  41.0 2.8 copy.21
  44.0 0.3 fusion.29
  44.3 0.2 fusion.18
  44.5 1.1 convolution_bitcast_fusion
  45.6 38.5 %all-gather.7.cloned.1.call-done = bf16[1,10240,256]{2,1,0:T(8,128)(2,1)} async-done(((bf16[1,320,256]{2,1,0:T(8,128)(2,1)}), bf16[1,10240,256]{2,1,0:T(8,128)(2,1)}) %all-gather.7.cloned.1.call-update) | async-done | bytes 5242896 | tf_op jit(solution)/shard_map/all_gather | solution.py:42
  84.1 70.4 %all-gather.5.cloned.1.call-done = bf16[1,10240,256]{2,1,0:T(8,128)(2,1)} async-done(((bf16[1,320,256]{2,1,0:T(8,128)(2,1)}), bf16[1,10240,256]{2,1,0:T(8,128)(2,1)}) %all-gather.5.cloned.1.call-update) | async-done | bytes 5242896 | tf_op jit(solution)/shard_map/all_gather | solution.py:41
  154.5 59.6 %while.19 = (s32[]{:T(128)}, f32[320,2]{0,1:T(2,128)S(1)}, f32[320,2]{0,1:T(2,128)S(1)}, f32[320,2,128]{2,0,1:T(8,128)}, s32[]{:T(128)}, /*index=5*/bf16[10240,2...) while((s32[]{:T(128)}, f32[320,2]{0,1:T(2,128)S(1)}, ...), condition=%wide.region_5.6_spmd, body=%wide.region_2.5_spmd.sunk | while | flops 685692160 | bytes 33898752 | solution.py:70
  154.5 2.7 constant_dynamic-slice_fusion.3
  157.2 2.3 copy.52
  159.5 1.4 copy.53
  160.9 2.3 bitcast_reduce_fusion.2
  163.2 1.1 fusion.48
  164.4 1.3 fusion.49
  165.7 0.0 copy-start.3
  165.7 0.7 copy-done.3
  166.4 2.7 constant_dynamic-slice_fusion.3
  169.1 2.3 copy.52
  171.4 1.4 copy.53
  172.8 2.3 bitcast_reduce_fusion.2
  175.2 1.1 fusion.48
  176.3 1.3 fusion.49
  177.6 0.0 copy-start.3
  177.6 0.7 copy-done.3
  178.3 2.7 constant_dynamic-slice_fusion.3
  181.0 2.3 copy.52
  183.3 1.4 copy.53
  184.7 2.3 bitcast_reduce_fusion.2
  187.1 1.1 fusion.48
  188.2 0.0 copy-done.1
  188.2 1.3 fusion.49
  189.5 0.0 copy-start.3
  189.5 0.7 copy-done.3
  190.3 2.7 constant_dynamic-slice_fusion.3
  192.9 2.3 copy.52
  195.2 1.4 copy.53
  196.6 2.3 bitcast_reduce_fusion.2
  199.0 1.1 fusion.48
  200.2 1.3 fusion.49
  201.4 0.0 copy-start.3
  201.5 0.7 copy-done.3
  202.2 2.7 constant_dynamic-slice_fusion.3
  204.9 2.3 copy.52
  207.1 1.4 copy.53
  208.6 2.3 bitcast_reduce_fusion.2
  210.9 1.1 fusion.48
  212.1 1.3 fusion.49
  213.3 0.0 copy-start.3
  213.4 0.7 copy-done.3
  214.1 3.0 %convolution_convert_fusion = bf16[320,3072]{1,0:T(8,128)(2,1)} fusion(bf16[256,3072]{1,0:T(8,128)(2,1)S(1)} %copy-done, f32[320,2,128]{2,0,1:T(8,128)} %get-tuple-element.202, f32[320,2]{0,1:T(2,128)S(1)} %get-tuple-element.203), kind=kOutput, calls=%fused_computation.22 | convolution fusion | flops 504463360 | bytes 3869184 | tf_op jit(solution)/shard_map/dot_general | solution.py:75
  217.1 0.0 reduce-scatter.2.cloned.1.call-update
  217.1 0.7 slice.34
  217.9 77.8 %reduce-scatter.2.cloned.1.call-done = bf16[40,3072]{1,0:T(8,128)(2,1)} async-done(((bf16[320,3072]{1,0:T(8,128)(2,1)}), bf16[40,3072]{1,0:T(8,128)(2,1)}) %reduce-scatter.2.cloned.1.call-update) | async-done | bytes 245776 | tf_op jit(solution)/shard_map/reduce_scatter | solution.py:74
  (45 shorter events, 0.4 us)
Async XLA Ops:
  7.2 206.9 %copy-start = (bf16[256,3072]{1,0:T(8,128)(2,1)S(1)}, bf16[256,3072]{1,0:T(8,128)(2,1)}, u32[]{:S(2)}) copy-start(bf16[256,3072]{1,0:T(8,128)(2,1)} %param.7) | copy-start | bytes 4718596
  7.2 76.9 %all-gather.7.cloned.1.call-start = ((), (), s32[]{:S(2)}) async-start(), calls=%async_computation.4 | async-start | bytes 5406720 | tf_op jit(solution)/shard_map/all_gather | solution.py:42
  9.1 145.4 %all-gather.5.cloned.1.call-start = ((), (), s32[]{:S(2)}) async-start(), calls=%async_computation.3 | async-start | bytes 5406720 | tf_op jit(solution)/shard_map/all_gather | solution.py:41
  18.6 18.8 %all-to-all-start = ((bf16[8,2,15360]{2,1,0:T(2,128)(2,1)}), bf16[8,2,15360]{2,1,0:T(2,128)(2,1)S(1)}, u32[]{:S(2)}, u32[]{:S(2)}) async-start(bf16[8,2,15360]{2,1,0:T(2,128)(2,1)} %reshape.54), calls=%async_computation | async-start | bytes 983040 | tf_op jit(solution)/shard_map/all_to_all | solution.py:22
  26.1 269.6 %reduce-scatter.2.cloned.1.call-start = ((), (), s32[]{:S(2)}) async-start(), calls=%async_computation.2 | async-start | bytes 2211840 | tf_op jit(solution)/shard_map/reduce_scatter | solution.py:74
  160.9 3.5 %copy-start.1 = (bf16[2048,256]{0,1:T(8,128)(2,1)S(1)}, bf16[2048,256]{0,1:T(8,128)(2,1)}, u32[]{:S(2)}) copy-start(bf16[2048,256]{0,1:T(8,128)(2,1)} %copy.53) | copy-start | bytes 3145732 | tf_op jit(solution)/shard_map/while
  160.9 3.5 %copy-start.2 = (f32[320,2,128]{2,0,1:T(8,128)S(1)}, f32[320,2,128]{2,0,1:T(8,128)}, u32[]{:S(2)}) copy-start(f32[320,2,128]{2,0,1:T(8,128)} %get-tuple-element.325) | copy-start | bytes 983044 | tf_op jit(solution)/shard_map/while
  165.7 0.7 copy-start.3
  172.8 3.5 %copy-start.1 = (bf16[2048,256]{0,1:T(8,128)(2,1)S(1)}, bf16[2048,256]{0,1:T(8,128)(2,1)}, u32[]{:S(2)}) copy-start(bf16[2048,256]{0,1:T(8,128)(2,1)} %copy.53) | copy-start | bytes 3145732 | tf_op jit(solution)/shard_map/while
  172.8 3.5 %copy-start.2 = (f32[320,2,128]{2,0,1:T(8,128)S(1)}, f32[320,2,128]{2,0,1:T(8,128)}, u32[]{:S(2)}) copy-start(f32[320,2,128]{2,0,1:T(8,128)} %get-tuple-element.325) | copy-start | bytes 983044 | tf_op jit(solution)/shard_map/while
  177.6 0.7 copy-start.3
  184.7 3.5 %copy-start.1 = (bf16[2048,256]{0,1:T(8,128)(2,1)S(1)}, bf16[2048,256]{0,1:T(8,128)(2,1)}, u32[]{:S(2)}) copy-start(bf16[2048,256]{0,1:T(8,128)(2,1)} %copy.53) | copy-start | bytes 3145732 | tf_op jit(solution)/shard_map/while
  184.7 3.5 %copy-start.2 = (f32[320,2,128]{2,0,1:T(8,128)S(1)}, f32[320,2,128]{2,0,1:T(8,128)}, u32[]{:S(2)}) copy-start(f32[320,2,128]{2,0,1:T(8,128)} %get-tuple-element.325) | copy-start | bytes 983044 | tf_op jit(solution)/shard_map/while
  189.5 0.7 copy-start.3
  196.6 3.5 %copy-start.1 = (bf16[2048,256]{0,1:T(8,128)(2,1)S(1)}, bf16[2048,256]{0,1:T(8,128)(2,1)}, u32[]{:S(2)}) copy-start(bf16[2048,256]{0,1:T(8,128)(2,1)} %copy.53) | copy-start | bytes 3145732 | tf_op jit(solution)/shard_map/while
  196.6 3.5 %copy-start.2 = (f32[320,2,128]{2,0,1:T(8,128)S(1)}, f32[320,2,128]{2,0,1:T(8,128)}, u32[]{:S(2)}) copy-start(f32[320,2,128]{2,0,1:T(8,128)} %get-tuple-element.325) | copy-start | bytes 983044 | tf_op jit(solution)/shard_map/while
  201.4 0.7 copy-start.3
  208.6 3.5 %copy-start.1 = (bf16[2048,256]{0,1:T(8,128)(2,1)S(1)}, bf16[2048,256]{0,1:T(8,128)(2,1)}, u32[]{:S(2)}) copy-start(bf16[2048,256]{0,1:T(8,128)(2,1)} %copy.53) | copy-start | bytes 3145732 | tf_op jit(solution)/shard_map/while
  208.6 3.5 %copy-start.2 = (f32[320,2,128]{2,0,1:T(8,128)S(1)}, f32[320,2,128]{2,0,1:T(8,128)}, u32[]{:S(2)}) copy-start(f32[320,2,128]{2,0,1:T(8,128)} %get-tuple-element.325) | copy-start | bytes 983044 | tf_op jit(solution)/shard_map/while
  213.3 0.7 copy-start.3
Sparse Core Ops, SparseCore 0:
  10.4 73.5 all-gather.6
  85.9 68.5 all-gather.4
  217.2 78.3 reduce-scatter.1
where the time goes:
time: 303 us; the launch traced here: 302 us
  waiting for transfers between devices  199 us (66%)
  local copies, waits for them, and re-layouts  53.4 us (18%)
  matrix products  22.4 us (7%)
  between operations  13.8 us (5%)
  starting transfers between devices  7.6 us (3%)
  other arithmetic  6.06 us (2%)
    reduce_scatter x1, waiting for transfers between devices, on_device(): lax.psum_scatter(jnp.dot(attended, out_weight, preferred_element_type=jnp...  77.8 us
    all_gather x1, waiting for transfers between devices, on_device(): key_rows = lax.all_gather(stale_kv[0], 'patch', axis=0, tiled=True)  70.4 us
    all_gather x1, waiting for transfers between devices, on_device(): value_rows = lax.all_gather(stale_kv[1], 'patch', axis=0, tiled=True)  38.5 us
    dynamic_slice x10, local copies, waits for them, and re-layouts, advance(): lax.dynamic_slice_in_dim(value_rows, block_offset, block_size, 0)  20.5 us
    unnamed x5, local copies, waits for them, and re-layouts  12.3 us
    dot_general x6, matrix products, score_block(): jnp.einsum('qhd,khd->qhk', queries, key_block, preferred_element_type=jnp...  11.9 us
    dynamic_slice x5, local copies, waits for them, and re-layouts, advance(): key_block = lax.dynamic_slice_in_dim(key_rows, block_offset, block_size, 0)  11.3 us
    all_to_all x1, waiting for transfers between devices, on_device(): lax.all_to_all(qkv, 'uly', split_axis=2, concat_axis=1, tiled=True)  11.3 us
  transfers between devices with their start and end apart: 4, of which 4 were waited for; matrix products, arithmetic and copies ran while one was open for 6% of the time, Pallas kernels for 0%

commit v1 on v0

v1 whole, which is shorter than its diff:
```python
import functools

import jax
import jax.numpy as jnp
from jax import lax
from jax.experimental import pallas as pl
from jax.experimental.pallas import tpu as pltpu
from jax.sharding import PartitionSpec as P

MESH = pl.DeviceIdType.MESH
HD = 128
NZ = 8
NU = 8
TOK = 40
GRP = 320
PAIR = 640
HALF = 160
D = 3072
STEPS = 14
SCALE = HD ** -0.5 * 1.4426950408889634
NT = (((1,), (1,)), ((), ()))
F32 = jnp.float32
BF16 = jnp.bfloat16
W1, W2 = 18, 24
CHUNK = 512


def rows(offset, size, unit=16):
    return pl.ds(pl.multiple_of(offset, unit), size)


def kernel(
    qkv_ref, stale_ref, w_ref, mixed_ref, fresh_ref,
    kv, fr, q, s, p, m, l, acc, qs, kvs, qr, kvr, wg, stat_out, stat_in,
    osend, orecv, bsend, brecv, afin,
    local_sem, ring_s, ring_r, sib_s, sib_r, own_s, own_r, q_s, q_r, f_s, f_r,
    w_s, w_r, wb_s, wb_r, st_s, st_r, o_s, o_r, b_s, b_r,
):
    pi, u = lax.axis_index("patch"), lax.axis_index("uly")
    z, yl, c = pi // 4, (pi // 2) % 2, pi % 2
    yh, x = u // 4, u % 4

    def patch(z_, yl_, c_):
        return z_ * 4 + yl_ * 2 + c_

    sibling = (patch(z, yl, 1 - c), u)
    up = (patch((z + 1) % NZ, yl, c), u)
    down = (patch((z + 7) % NZ, yl, c), u)
    x_up = (pi, yh * 4 + (x + 1) % 4)
    x_down = (pi, yh * 4 + (x + 3) % 4)
    other = patch(z, 1 - yl, c)

    barrier = pltpu.get_barrier_semaphore()
    everyone = [sibling, up, down]
    everyone += [(pi, (u + k) % NU) for k in range(1, NU)]
    everyone += [(other, (u + k) % NU) for k in range(NU)]
    for device in everyone:
        pl.semaphore_signal(barrier, inc=1, device_id=device, device_id_type=MESH)

    def remote(src, dst, send, recv, device):
        return pltpu.make_async_remote_copy(
            src_ref=src, dst_ref=dst, send_sem=send, recv_sem=recv, device_id=device, device_id_type=MESH
        )

    mine = rows(c * GRP, GRP)
    locals_ = []
    for kind in range(4):
        locals_.append(pltpu.make_async_copy(
            stale_ref.at[kind // 2, :, pl.ds(kind % 2 * HD, HD)], kv.at[kind, z, mine, :], local_sem.at[kind]
        ))
    w_local = pltpu.make_async_copy(w_ref, wg.at[rows(x * 2 * HD, 2 * HD), :], local_sem.at[4])
    for copy in locals_:
        copy.start()
    w_local.start()

    for v in range(NU):
        parts = [
            qkv_ref[i, :, pl.ds(v * 2 * HD + h * HD, HD)].astype(F32) for i in range(3) for h in range(2)
        ]
        qs[v] = jnp.concatenate(parts[:2], axis=0).astype(BF16)
        kvs[v] = jnp.concatenate(parts[2:], axis=0).astype(BF16)
    qr[0, u] = qs[u]
    kvr[u] = kvs[u]
    m[...] = jnp.full(m.shape, -jnp.inf, F32)
    l[...] = jnp.zeros(l.shape, F32)
    acc[...] = jnp.zeros(acc.shape, F32)
    for copy in locals_:
        copy.wait()
    w_local.wait()
    pl.semaphore_wait(barrier, len(everyone))

    def part(n, hops_before):
        phase, j = n // STEPS, n % STEPS
        hop, i = j // 4, j % 4
        head, half = i // 2, i % 2
        span = rows(c * GRP + half * HALF, HALF)
        right = kv.at[phase * 2 + head, (z + NZ - hop - hops_before) % NZ, span, :]
        left = kv.at[phase * 2 + 1 - head, (z + hop + hops_before) % NZ, span, :]
        return right, left

    def ring_copies(n, hops_before):
        right, left = part(n, hops_before)
        return (
            remote(right, right, ring_s.at[0, n], ring_r.at[0, n], up),
            remote(left, left, ring_s.at[1, n], ring_r.at[1, n], down),
        )

    def sib_copies(n):
        right, left = part(n, 1)
        return (
            remote(right, right, sib_s.at[0, n], sib_r.at[0, n], sibling),
            remote(left, left, sib_s.at[1, n], sib_r.at[1, n], sibling),
        )

    def sib_wait(n):
        phase, j = n // STEPS, n % STEPS
        hop, i = j // 4, j % 4
        head, half = i // 2, i % 2
        span = rows((1 - c) * GRP + half * HALF, HALF)
        right = kv.at[phase * 2 + head, (z + NZ - hop - 1) % NZ, span, :]
        left = kv.at[phase * 2 + 1 - head, (z + hop + 1) % NZ, span, :]
        remote(right, right, sib_s.at[0, n], sib_r.at[0, n], sibling).wait_recv()
        remote(left, left, sib_s.at[1, n], sib_r.at[1, n], sibling).wait_recv()

    for n in range(4):
        for copy in ring_copies(n, 0):
            copy.start()
    own_sib = remote(kv.at[:, z, mine, :], kv.at[:, z, mine, :], own_s.at[0], own_r.at[0], sibling)
    own_sib.start()

    def q_copies():
        copies = []
        for k in range(1, NU):
            v = (u + k) % NU
            copies.append((remote(qs.at[v], qr.at[0, u], q_s.at[0, k], q_r.at[0, u], (pi, v)), qr.at[0, v], q_r.at[0, v]))
        for k in range(NU):
            v = (u + k) % NU
            copies.append((remote(qs.at[v], qr.at[1, u], q_s.at[1, k], q_r.at[1, u], (other, v)), qr.at[1, v], q_r.at[1, v]))
        return copies

    def f_copies():
        copies = []
        for k in range(1, NU):
            v = (u + k) % NU
            copies.append((remote(kvs.at[v], kvr.at[u], f_s.at[k], f_r.at[u], (pi, v)), kvr.at[v], f_r.at[v]))
        return copies

    for copy, _, _ in q_copies():
        copy.start()

    def w_piece(direction, n):
        if direction == 0:
            origin, half = (x + 3 - n // 2) % 4, n % 2
        else:
            origin, half = (x + 1 + n // 2) % 4, 1 - n % 2
        return origin, half

    def w_slot(origin, half, core):
        return wg.at[rows(origin * 2 * HD + core * HD + half * 64, 64), :]

    def w_send(direction, n):
        if direction == 0:
            slot = w_slot((x + 4 - n // 2) % 4, n % 2, c)
            return remote(slot, slot, w_s.at[0, n], w_r.at[0, n], x_up)
        slot = w_slot((x + n // 2) % 4, 1 - n % 2, c)
        return remote(slot, slot, w_s.at[1, n], w_r.at[1, n], x_down)

    def w_wait(direction, n):
        slot = w_slot(*w_piece(direction, n), c)
        remote(slot, slot, w_s.at[direction, n], w_r.at[direction, n], x_up).wait_recv()

    def w_sib(direction, n, core):
        slot = w_slot(*w_piece(direction, n), core)
        return remote(slot, slot, wb_s.at[direction, n], wb_r.at[direction, n], sibling)

    for n in range(2):
        for direction in range(2):
            w_send(direction, n).start()
    for copy, _, _ in f_copies():
        copy.start()

    def assemble_queries():
        for _, slot, sem in q_copies():
            remote(slot, slot, q_s.at[0, 0], sem, sibling).wait_recv()
        for g in range(2):
            got = [qr[g, v].astype(F32) for v in range(NU)]
            for h in range(2):
                q[h, pl.ds(g * GRP, GRP), :] = jnp.concatenate(
                    [t[h * TOK:(h + 1) * TOK] for t in got], axis=0
                ).astype(BF16)

    def assemble_fresh():
        for _, slot, sem in f_copies():
            remote(slot, slot, f_s.at[0], sem, sibling).wait_recv()
        got = [kvr[v].astype(F32) for v in range(NU)]
        for kind in range(4):
            whole = jnp.concatenate([t[kind * TOK:(kind + 1) * TOK] for t in got], axis=0).astype(BF16)
            fr[kind, mine, :] = whole
            fresh_ref[kind // 2, :, pl.ds(kind % 2 * HD, HD)] = whole
        theirs = rows((1 - c) * GRP, GRP)
        remote(kv.at[:, z, theirs, :], kv.at[:, z, theirs, :], own_s.at[0], own_r.at[0], sibling).wait_recv()
        for kind in range(4):
            fr[kind, theirs, :] = kv[kind, z, theirs, :]

    def note_max(h, span, scores):
        best = m[h, span, :]
        for t in range(PAIR // HD):
            best = jnp.maximum(best, scores[:, t * HD:(t + 1) * HD])
        m[h, span, :] = best

    def score(h, zz):
        scores = lax.dot_general(q[h], kv[h, zz], NT, preferred_element_type=F32)
        s[h, zz] = scores
        note_max(h, slice(None), scores)

    def score_own(h):
        for g, keys in ((0, fr.at[h]), (1, kv.at[h, z])):
            span = pl.ds(g * GRP, GRP)
            scores = lax.dot_general(q[h, span, :], keys[...], NT, preferred_element_type=F32)
            s[h, z, span, :] = scores
            note_max(h, span, scores)

    def weigh(h, zz):
        top, total = m[h], l[h]
        for t in range(PAIR // HD):
            span = pl.ds(t * HD, HD)
            weight = jnp.exp2(s[h, zz, :, span] * SCALE - top)
            total = total + weight
            p[h, zz, :, span] = weight.astype(BF16)
        l[h] = total

    def attend(h, zz):
        acc[h] += jnp.dot(p[h, zz], kv[2 + h, zz], preferred_element_type=F32)

    def attend_own(h):
        for g, values in ((0, fr.at[2 + h]), (1, kv.at[2 + h, z])):
            span = pl.ds(g * GRP, GRP)
            acc[h, span, :] += jnp.dot(p[h, z, span, :], values[...], preferred_element_type=F32)

    def pair(t):
        hop, head = (t - 1) // 2, (t - 1) % 2
        return (z + 7 - hop) % NZ, (z + 1 + hop) % NZ, head

    def pair_arrived(phase, t):
        n = phase * STEPS + 2 * (t - 1)
        sib_wait(n)
        sib_wait(n + 1)

    def score_pair(t):
        pair_arrived(0, t)
        z0, z1, head = pair(t)
        score(head, z0)
        score(1 - head, z1)

    def attend_pair(t):
        pair_arrived(1, t)
        z0, z1, head = pair(t)
        attend(head, z0)
        attend(1 - head, z1)

    def top_of_rows():
        for h in range(2):
            top = jnp.max(m[h], axis=1, keepdims=True) * SCALE
            m[h] = jnp.broadcast_to(top, (PAIR, HD))

    lane = lax.broadcasted_iota(jnp.int32, (PAIR, HD), 1)

    def stat_copy():
        return remote(stat_out, stat_in, st_s.at[0], st_r.at[0], (other, u))

    def send_stats():
        packed = jnp.zeros((PAIR, HD), F32)
        for h in range(2):
            total = jnp.broadcast_to(jnp.sum(l[h], axis=1, keepdims=True), (PAIR, HD))
            l[h] = total
            packed = jnp.where(lane == 2 * h, m[h], packed)
            packed = jnp.where(lane == 2 * h + 1, total, packed)
        stat_out[...] = packed.T[:8]
        stat_copy().start()

    def take_stats():
        stat_copy().wait_recv()
        got = jnp.concatenate([stat_in[...], jnp.zeros((HD - 8, PAIR), F32)], axis=0).T
        got = jnp.concatenate([got[GRP:], got[:GRP]], axis=0)
        for h in range(2):
            top, total = got[:, 2 * h:2 * h + 1], got[:, 2 * h + 1:2 * h + 2]
            mine_top, mine_total = m[h], l[h]
            most = jnp.maximum(mine_top, top)
            own = jnp.exp2(mine_top - most)
            l[h] = own / (mine_total * own + total * jnp.exp2(top - most))

    def body(n, _):
        for direction in range(2):
            arrived = ring_copies(n, 1)[direction]
            arrived.wait_recv()

            @pl.when(n + 4 < 2 * STEPS)
            def _():
                ring_copies(n + 4, 0)[direction].start()

            sib_copies(n)[direction].start()

        @pl.when(n == 4)
        def _():
            assemble_queries()

        @pl.when(n == 5)
        def _():
            assemble_fresh()
            lax.fori_loop(0, 2, lambda h, _: (score_own(h), 0)[1], 0)

        @pl.when(((n >= 6) & (n <= 9)) | (n == 11) | (n == 13) | (n == 15))
        def _():
            score_pair(jnp.where(n <= 9, n - 5, (n - 1) // 2))

        @pl.when(n == 16)
        def _():
            top_of_rows()

        @pl.when((n >= 16) & (n <= 19))
        def _():
            def one(k, _):
                weigh(k % 2, (n - 16) * 2 + k // 2)
                return 0

            lax.fori_loop(0, 4, one, 0)

        @pl.when(n == 19)
        def _():
            send_stats()

        @pl.when(n == 20)
        def _():
            lax.fori_loop(0, 2, lambda h, _: (attend_own(h), 0)[1], 0)

        @pl.when((n >= 21) & (n <= 25) | (n == 27))
        def _():
            attend_pair(jnp.where(n <= 25, n - 20, 6))

        @pl.when(n == W1)
        def _():
            for direction in range(2):
                w_wait(direction, 0)
                w_send(direction, 2).start()
                w_sib(direction, 0, c).start()

        @pl.when(n == W2)
        def _():
            for direction in range(2):
                w_wait(direction, 1)
                w_sib(direction, 1, c).start()

        @pl.when(n == 26)
        def _():
            take_stats()

        return 0

    lax.fori_loop(0, 2 * STEPS, body, 0)
    attend_pair(jnp.int32(7))

    for h in range(2):
        acc[h] = acc[h] * l[h]

    def o_block(same, xt):
        mine_rows, other_rows = (0, GRP) if same else (GRP, 0)
        a = mine_rows + TOK * (4 * yh + xt)
        b = other_rows + TOK * (4 * (1 - yh) + xt)
        return jnp.concatenate(
            [acc[h, rows(r, TOK, 8), :] for r in (a, b) for h in range(2)], axis=0
        ).astype(BF16)

    def o_copy(same, dx):
        xt = (x + dx) % 4
        k = (0 if same else 4) + dx
        return remote(
            osend.at[k], orecv.at[yl * 4 + x], o_s.at[k], o_r.at[yl * 4 + x],
            (pi if same else other, yh * 4 + xt),
        )

    order = [(False, 2), (True, 2), (False, 1), (False, 3), (True, 1), (True, 3), (False, 0)]
    for same, dx in order:
        k = (0 if same else 4) + dx
        osend[k] = o_block(same, (x + dx) % 4)
        o_copy(same, dx).start()
    orecv[yl * 4 + x] = o_block(True, x)

    for direction in range(2):
        w_wait(direction, 2)
        w_sib(direction, 2, c).start()
    for direction in range(2):
        for n in range(3):
            w_sib(direction, n, 1 - c).wait_recv()

    for same, dx in order:
        slot = (yl if same else 1 - yl) * 4 + (x + dx) % 4
        remote(orecv.at[slot], orecv.at[slot], o_s.at[0], o_r.at[slot], sibling).wait_recv()
    columns = []
    for sx in range(4):
        both = orecv[sx].astype(F32) + orecv[4 + sx].astype(F32)
        for h in range(2):
            columns.append(jnp.concatenate(
                [both[h * TOK:(h + 1) * TOK], both[(2 + h) * TOK:(3 + h) * TOK]], axis=0
            ))
    attended = jnp.concatenate(columns, axis=1).astype(BF16)

    facing = (other, (1 - yh) * 4 + x)

    def b_copy(n):
        span = pl.ds(n * HALF, HALF)
        return remote(bsend.at[span, :], brecv.at[span, :], b_s.at[n], b_r.at[n], facing)

    for n in range(D // CHUNK):
        got = jnp.dot(attended, wg[:, pl.ds(n * CHUNK, CHUNK)], preferred_element_type=F32)
        bsend[pl.ds(n * HALF, HALF), :] = jnp.concatenate(
            [got[TOK:, t * HD:(t + 1) * HD] for t in range(CHUNK // HD)], axis=0
        ).astype(BF16)
        b_copy(n).start()
        afin[:, pl.ds(n * CHUNK, CHUNK)] = got[:TOK]
    for n in range(D // CHUNK):
        b_copy(n).wait_recv()
        theirs = brecv[pl.ds(n * HALF, HALF), :].astype(F32)
        theirs = jnp.concatenate([theirs[t * TOK:(t + 1) * TOK] for t in range(CHUNK // HD)], axis=1)
        span = pl.ds(n * CHUNK, CHUNK)
        mixed_ref[:, span] = (afin[:, span] + theirs).astype(BF16)

    def sent(n, _):
        for copy in ring_copies(n, 0) + sib_copies(n):
            copy.wait_send()
        return 0

    lax.fori_loop(0, 2 * STEPS, sent, 0)
    own_sib.wait_send()
    for copy, _, _ in q_copies() + f_copies():
        copy.wait_send()
    for direction in range(2):
        for n in range(3):
            w_send(direction, n).wait_send()
            w_sib(direction, n, c).wait_send()
    stat_copy().wait_send()
    for same, dx in order:
        o_copy(same, dx).wait_send()
    for n in range(D // CHUNK):
        b_copy(n).wait_send()


def on_device(qkv, stale_kv, out_weight):
    vmem = pl.BlockSpec(memory_space=pltpu.VMEM)
    dma = pltpu.SemaphoreType.DMA
    return pl.pallas_call(
        kernel,
        out_shape=(
            jax.ShapeDtypeStruct((TOK, D), BF16),
            jax.ShapeDtypeStruct((2, GRP, 2 * HD), BF16),
        ),
        in_specs=[vmem, vmem, pl.BlockSpec(memory_space=pl.ANY)],
        out_specs=(vmem, vmem),
        scratch_shapes=[
            pltpu.VMEM((4, NZ, PAIR, HD), BF16),
            pltpu.VMEM((4, PAIR, HD), BF16),
            pltpu.VMEM((2, PAIR, HD), BF16),
            pltpu.VMEM((2, NZ, PAIR, PAIR), F32),
            pltpu.VMEM((2, NZ, PAIR, PAIR), BF16),
            pltpu.VMEM((2, PAIR, HD), F32),
            pltpu.VMEM((2, PAIR, HD), F32),
            pltpu.VMEM((2, PAIR, HD), F32),
            pltpu.VMEM((NU, 2 * TOK, HD), BF16),
            pltpu.VMEM((NU, 4 * TOK, HD), BF16),
            pltpu.VMEM((2, NU, 2 * TOK, HD), BF16),
            pltpu.VMEM((NU, 4 * TOK, HD), BF16),
            pltpu.VMEM((8 * HD, D), BF16),
            pltpu.VMEM((8, PAIR), F32),
            pltpu.VMEM((8, PAIR), F32),
            pltpu.VMEM((8, 4 * TOK, HD), BF16),
            pltpu.VMEM((8, 4 * TOK, HD), BF16),
            pltpu.VMEM((TOK * D // HD, HD), BF16),
            pltpu.VMEM((TOK * D // HD, HD), BF16),
            pltpu.VMEM((TOK, D), F32),
            dma((5,)),
            dma((2, 2 * STEPS)), dma((2, 2 * STEPS)), dma((2, 2 * STEPS)), dma((2, 2 * STEPS)),
            dma((1,)), dma((1,)),
            dma((2, NU)), dma((2, NU)), dma((NU,)), dma((NU,)),
            dma((2, 3)), dma((2, 3)), dma((2, 3)), dma((2, 3)),
            dma((1,)), dma((1,)),
            dma((8,)), dma((8,)), dma((D // CHUNK,)), dma((D // CHUNK,)),
        ],
        compiler_params=pltpu.CompilerParams(
            collective_id=0, has_side_effects=True, vmem_limit_bytes=62 * 2**20
        ),
    )(qkv, stale_kv, out_weight)


def solution(mesh):
    placed = (P(None, ("patch", "uly"), None), P(None, "patch", "uly"), P("uly", None))
    return jax.shard_map(
        on_device,
        mesh=mesh,
        in_specs=placed,
        out_specs=(P(("patch", "uly"), None), P(None, "patch", "uly")),
        check_vma=False,
    )
```

time: 303 us -> 86.8 us (0.29)
  waiting for transfers between devices: 199 us -> 0 us
  Pallas kernels: 0 us -> 82.6 us
  local copies, waits for them, and re-layouts: 53.4 us -> 3.37 us
  matrix products: 22.4 us -> 0 us
  between operations: 13.8 us -> 0.64 us
  starting transfers between devices: 7.6 us -> 0 us
  other arithmetic: 6.06 us -> 0 us
    all_gather x2 -> x0, waiting for transfers between devices: 109 us -> none  [the longest x1 70.4 us: on_device(): key_rows = lax.all_gather(stale_kv[0], 'patch', axis=0, tiled=True)]
    pallas_call x0 -> x1, Pallas kernels: none -> 82.6 us  [on_device(): pl.pallas_call(kernel, out_shape=(jax.ShapeDtypeStruct((TOK, D), BF16), j...]
    reduce_scatter x1 -> x0, waiting for transfers between devices: 77.8 us -> none  [on_device(): lax.psum_scatter(jnp.dot(attended, out_weight, preferred_element_type=jnp...]
    dynamic_slice x15 -> x0, local copies, waits for them, and re-layouts: 31.9 us -> none  [the longest x10 20.5 us: advance(): lax.dynamic_slice_in_dim(value_rows, block_offset, block_size, 0)]
    dot_general x13 -> x0, matrix products: 22.4 us -> none  [the longest x6 11.9 us: score_block(): jnp.einsum('qhd,khd->qhk', queries, key_block, preferred_element_type=jnp...]
    all_to_all x1 -> x0, waiting for transfers between devices: 11.3 us -> none  [on_device(): lax.all_to_all(qkv, 'uly', split_axis=2, concat_axis=1, tiled=True)]
    unnamed x5 -> x2, local copies, waits for them, and re-layouts: 12.3 us -> 3.37 us
    all_to_all x1 -> x0, starting transfers between devices: 7.48 us -> none  [on_device(): lax.all_to_all(qkv, 'uly', split_axis=2, concat_axis=1, tiled=True)]
  transfers between devices with their start and end apart: 4 -> 0, of which waited for: 4 -> 0; matrix products, arithmetic and copies ran while one was open for 6% -> 0% of each run, Pallas kernels for 0% -> 0%
where the time goes in v1:
time: 86.8 us; the launch traced here: 86.6 us
  Pallas kernels  82.6 us (95%)
  local copies, waits for them, and re-layouts  3.37 us (4%)
    pallas_call x1, Pallas kernels, on_device(): pl.pallas_call(kernel, out_shape=(jax.ShapeDtypeStruct((TOK, D), BF16), j...  82.6 us
    unnamed x2, local copies, waits for them, and re-layouts  3.37 us

profile of v1, /device:TPU:1, one launch (start us, length us, event | category | flops | bytes accessed | tf_op | source)
XLA Modules:
  0.0 86.6 jit_solution(10096609383956976684)
XLA Ops:
  0.6 82.6 %shard_map.50 = (bf16[40,3072]{1,0:T(8,128)(2,1)}, bf16[2,320,256]{2,1,0:T(8,128)(2,1)}) custom-call(bf16[3,40,2048]{2,1,0:T(8,128)(2,1)} %qkv_ref.1, bf16[2,320,256]{2,1,0:T(8,128)(2,1)} %stale_ref.1, bf16[256,3072]{1,0:T(8,128)(2,1)} %w_ref.1), custom_call_target="tpu_custom_call" | custom-call | tf_op jit(solution)/shard_map/pallas_call | solution.py:450
  83.2 1.7 %copy.7 = bf16[40,3072]{1,0:T(8,128)(2,1)} copy(bf16[40,3072]{1,0:T(8,128)(2,1)} %get-tuple-element.4) | data formatting | bytes 491520
  84.9 1.7 %copy.8 = bf16[2,320,256]{2,1,0:T(8,128)(2,1)} copy(bf16[2,320,256]{2,1,0:T(8,128)(2,1)} %get-tuple-element.5) | data formatting | bytes 655360

commit v2 on v1

v2 whole, which is shorter than its diff:
```python
import functools

import jax
import jax.numpy as jnp
from jax import lax
from jax.experimental import pallas as pl
from jax.experimental.pallas import tpu as pltpu
from jax.sharding import PartitionSpec as P

MESH = pl.DeviceIdType.MESH
HD = 128
NZ = 8
NU = 8
TOK = 40
GRP = 320
PAIR = 640
HALF = 160
D = 3072
STEPS = 14
SCALE = HD ** -0.5 * 1.4426950408889634
NT = (((1,), (1,)), ((), ()))
F32 = jnp.float32
BF16 = jnp.bfloat16
W1, W2 = 13, 23
CHUNK = 512


def rows(offset, size, unit=16):
    return pl.ds(pl.multiple_of(offset, unit), size)


def kernel(
    qkv_ref, stale_ref, w_ref, mixed_ref, fresh_ref,
    qkv, kv, fr, q, s, p, m, top, fix, l, acc, qs, kvs, qr, kvr, wg, stat_out, stat_in,
    osend, orecv, bsend, brecv, afin, mixed, fresh,
    local_sem, ring_r, pass_s, sib_r, own_s, own_r, q_s, q_r, f_s, f_r,
    w_s, w_r, wb_r, st_s, st_r, o_s, o_r, b_s, b_r,
):
    pi, u = lax.axis_index("patch"), lax.axis_index("uly")
    z, yl, c = pi // 4, (pi // 2) % 2, pi % 2
    yh, x = u // 4, u % 4

    def patch(z_, yl_, c_):
        return z_ * 4 + yl_ * 2 + c_

    sibling = (patch(z, yl, 1 - c), u)
    up = (patch((z + 1) % NZ, yl, c), u)
    down = (patch((z + 7) % NZ, yl, c), u)
    x_up = (pi, yh * 4 + (x + 1) % 4)
    x_down = (pi, yh * 4 + (x + 3) % 4)
    other = patch(z, 1 - yl, c)

    barrier = pltpu.get_barrier_semaphore()
    everyone = [sibling, up, down]
    everyone += [(pi, (u + k) % NU) for k in range(1, NU)]
    everyone += [(other, (u + k) % NU) for k in range(NU)]
    for device in everyone:
        pl.semaphore_signal(barrier, inc=1, device_id=device, device_id_type=MESH)

    def remote(src, dst, send, recv, device):
        return pltpu.make_async_remote_copy(
            src_ref=src, dst_ref=dst, send_sem=send, recv_sem=recv, device_id=device, device_id_type=MESH
        )

    mine = rows(c * GRP, GRP)
    def wait(ref, sem):
        pltpu.make_async_copy(ref, ref, sem).wait()

    qkv_in = pltpu.make_async_copy(qkv_ref, qkv, local_sem.at[7])
    qkv_in.start()
    locals_ = []
    for kind in range(4):
        locals_.append(pltpu.make_async_copy(
            stale_ref.at[kind // 2, :, pl.ds(kind % 2 * HD, HD)], kv.at[kind, z, mine, :], local_sem.at[kind]
        ))
    w_local = pltpu.make_async_copy(w_ref, wg.at[rows(x * 2 * HD, 2 * HD), :], local_sem.at[4])
    for copy in locals_:
        copy.start()
    w_local.start()

    qkv_in.wait()
    for v in range(NU):
        parts = [
            qkv[i, :, pl.ds(v * 2 * HD + h * HD, HD)].astype(F32) for i in range(3) for h in range(2)
        ]
        qs[v] = jnp.concatenate(parts[:2], axis=0).astype(BF16)
        kvs[v] = jnp.concatenate(parts[2:], axis=0).astype(BF16)
    pltpu.make_async_copy(qs.at[u], qr.at[0, u], q_r.at[0]).start()
    pltpu.make_async_copy(kvs.at[u], kvr.at[u], f_r.at[0]).start()
    m[...] = jnp.full(m.shape, -jnp.inf, F32)
    l[...] = jnp.zeros(l.shape, F32)
    acc[...] = jnp.zeros(acc.shape, F32)
    for copy in locals_:
        copy.wait()
    w_local.wait()
    pl.semaphore_wait(barrier, len(everyone))

    def part(n, hops_before):
        phase, j = n // STEPS, n % STEPS
        hop, i = j // 4, j % 4
        head, half = i // 2, i % 2
        span = rows(c * GRP + half * HALF, HALF)
        right = kv.at[phase * 2 + head, (z + NZ - hop - hops_before) % NZ, span, :]
        left = kv.at[phase * 2 + 1 - head, (z + hop + hops_before) % NZ, span, :]
        return right, left

    def ring_copies(n, hops_before):
        for slot, device in zip(part(n, hops_before), (up, down)):
            yield remote(slot, slot, pass_s.at[0], ring_r.at[n], device)

    def sib_copies(n):
        for slot in part(n, 1):
            yield remote(slot, slot, pass_s.at[0], sib_r.at[n // 2], sibling)

    for n in range(4):
        for copy in ring_copies(n, 0):
            copy.start()
    own_sib = remote(kv.at[:, z, mine, :], kv.at[:, z, mine, :], own_s.at[0], own_r.at[0], sibling)
    own_sib.start()

    def q_copies():
        for g, where in ((0, pi), (1, other)):
            for k in range(1 - g, NU):
                v = (u + k) % NU
                yield remote(qs.at[v], qr.at[g, u], q_s.at[g], q_r.at[0], (where, v))

    def f_copies():
        for k in range(1, NU):
            v = (u + k) % NU
            yield remote(kvs.at[v], kvr.at[u], f_s.at[0], f_r.at[0], (pi, v))

    for copy in q_copies():
        copy.start()
    for copy in f_copies():
        copy.start()

    def w_piece(direction, n):
        if direction == 0:
            origin, half = (x + 3 - n // 2) % 4, n % 2
        else:
            origin, half = (x + 1 + n // 2) % 4, 1 - n % 2
        return origin, half

    def w_slot(origin, half, core):
        return wg.at[rows(origin * 2 * HD + core * HD + half * 64, 64), :]

    def w_send(direction, n):
        if direction == 0:
            slot = w_slot((x + 4 - n // 2) % 4, n % 2, c)
            return remote(slot, slot, w_s.at[0], w_r.at[0, n], x_up)
        slot = w_slot((x + n // 2) % 4, 1 - n % 2, c)
        return remote(slot, slot, w_s.at[0], w_r.at[1, n], x_down)

    def w_wait(direction, n):
        wait(w_slot(*w_piece(direction, n), c), w_r.at[direction, n])

    def w_sib(direction, n):
        slot = w_slot(*w_piece(direction, n), c)
        return remote(slot, slot, w_s.at[0], wb_r.at[0], sibling)

    for n in range(2):
        for direction in range(2):
            w_send(direction, n).start()
    def assemble_queries():
        wait(qr, q_r.at[0])
        for g in range(2):
            got = [qr[g, v].astype(F32) for v in range(NU)]
            for h in range(2):
                q[h, pl.ds(g * GRP, GRP), :] = jnp.concatenate(
                    [t[h * TOK:(h + 1) * TOK] for t in got], axis=0
                ).astype(BF16)

    fresh_out = pltpu.make_async_copy(fresh, fresh_ref, local_sem.at[5])
    mixed_out = pltpu.make_async_copy(mixed, mixed_ref, local_sem.at[6])

    def assemble_fresh():
        wait(kvr, f_r.at[0])
        got = [kvr[v].astype(F32) for v in range(NU)]
        for kind in range(4):
            whole = jnp.concatenate([t[kind * TOK:(kind + 1) * TOK] for t in got], axis=0).astype(BF16)
            fr[kind, mine, :] = whole
            fresh[kind // 2, :, pl.ds(kind % 2 * HD, HD)] = whole
        fresh_out.start()
        theirs = rows((1 - c) * GRP, GRP)
        wait(kv.at[:, z, theirs, :], own_r.at[0])
        for kind in range(4):
            fr[kind, theirs, :] = kv[kind, z, theirs, :]

    def note_max(h, span, scores):
        best = m[h, span, :]
        for t in range(PAIR // HD):
            best = jnp.maximum(best, scores[:, t * HD:(t + 1) * HD])
        m[h, span, :] = best

    def score(h, zz):
        scores = lax.dot_general(q[h], kv[h, zz], NT, preferred_element_type=F32)
        s[h, zz] = scores
        note_max(h, slice(None), scores)

    def score_own(h):
        for g, keys in ((0, fr.at[h]), (1, kv.at[h, z])):
            span = pl.ds(g * GRP, GRP)
            scores = lax.dot_general(q[h, span, :], keys[...], NT, preferred_element_type=F32)
            s[h, z, span, :] = scores
            note_max(h, span, scores)

    def weigh(h, zz):
        most, total = top[h], l[h]
        for t in range(PAIR // HD):
            span = pl.ds(t * HD, HD)
            weight = jnp.exp2(s[h, zz, :, span] * SCALE - most)
            total = total + weight
            p[h, zz, :, span] = weight.astype(BF16)
        l[h] = total

    def attend(h, zz):
        acc[h] += jnp.dot(p[h, zz], kv[2 + h, zz], preferred_element_type=F32)

    def attend_own(h):
        for g, values in ((0, fr.at[2 + h]), (1, kv.at[2 + h, z])):
            span = pl.ds(g * GRP, GRP)
            acc[h, span, :] += jnp.dot(p[h, z, span, :], values[...], preferred_element_type=F32)

    def pair(t):
        hop, head = (t - 1) // 2, (t - 1) % 2
        return (z + 7 - hop) % NZ, (z + 1 + hop) % NZ, head

    def pair_arrived(phase, t):
        wait(kv.at[0, 0], sib_r.at[phase * STEPS // 2 + t - 1])

    def score_pair(t):
        pair_arrived(0, t)
        z0, z1, head = pair(t)
        score(head, z0)
        score(1 - head, z1)

    def attend_pair(t):
        pair_arrived(1, t)
        z0, z1, head = pair(t)
        attend(head, z0)
        attend(1 - head, z1)

    def row_max(h):
        return jnp.broadcast_to(jnp.max(m[h], axis=1, keepdims=True) * SCALE, (PAIR, HD))

    def first_top():
        for h in range(2):
            top[h] = row_max(h)

    def last_top():
        for h in range(2):
            old, new = top[h], row_max(h)
            top[h] = new
            fix[h] = jnp.exp2(old - new)
            l[h] = l[h] * fix[h]

    def weigh_pair(t):
        z0, z1, head = pair(t)
        z0, z1, head = jnp.where(t == 0, z, z0), jnp.where(t == 0, z, z1), jnp.where(t == 0, 0, head)

        def one(k, _):
            weigh(jnp.where(k == 0, head, 1 - head), jnp.where(k == 0, z0, z1))
            return 0

        lax.fori_loop(0, 2, one, 0)

    lane = lax.broadcasted_iota(jnp.int32, (PAIR, HD), 1)

    def stat_copy():
        return remote(stat_out, stat_in, st_s.at[0], st_r.at[0], (other, u))

    def send_stats():
        packed = jnp.zeros((PAIR, HD), F32)
        for h in range(2):
            total = jnp.broadcast_to(jnp.sum(l[h], axis=1, keepdims=True), (PAIR, HD))
            l[h] = total
            packed = jnp.where(lane == 2 * h, top[h], packed)
            packed = jnp.where(lane == 2 * h + 1, total, packed)
        stat_out[...] = packed.T[:8]
        stat_copy().start()

    def take_stats():
        stat_copy().wait_recv()
        got = jnp.concatenate([stat_in[...], jnp.zeros((HD - 8, PAIR), F32)], axis=0).T
        got = jnp.concatenate([got[GRP:], got[:GRP]], axis=0)
        for h in range(2):
            their_top, total = got[:, 2 * h:2 * h + 1], got[:, 2 * h + 1:2 * h + 2]
            mine_top, mine_total = top[h], l[h]
            most = jnp.maximum(mine_top, their_top)
            own = jnp.exp2(mine_top - most)
            l[h] = own / (mine_total * own + total * jnp.exp2(their_top - most))

    def body(n, _):
        wait(kv.at[0, 0, pl.ds(0, GRP), :], ring_r.at[n])

        @pl.when(n + 4 < 2 * STEPS)
        def _():
            for copy in ring_copies(n + 4, 0):
                copy.start()

        for copy in sib_copies(n):
            copy.start()

        @pl.when(n == 2)
        def _():
            assemble_queries()

        @pl.when((n % 2 == 1) & (n >= 3) & (n <= 15))
        def _():
            score_pair((n - 1) // 2)

        @pl.when(n == 6)
        def _():
            assemble_fresh()
            lax.fori_loop(0, 2, lambda h, _: (score_own(h), 0)[1], 0)

        @pl.when(n == 10)
        def _():
            first_top()

        @pl.when(n == 16)
        def _():
            last_top()

        @pl.when(((n % 2 == 0) & (n >= 10) & (n <= 20)) | (n == 21) | (n == 22))
        def _():
            weigh_pair(jnp.where(n <= 20, (n - 10) // 2, n - 15))

        @pl.when(n == 22)
        def _():
            send_stats()

        @pl.when(n == 17)
        def _():
            lax.fori_loop(0, 2, lambda h, _: (attend_own(h), 0)[1], 0)

        @pl.when((n == 19) | (n >= 23))
        def _():
            attend_pair(jnp.where(n == 19, 1, n - 21))

        @pl.when(n == 23)
        def _():
            for h in range(2):
                acc[h] = acc[h] * fix[h]

        @pl.when(n == W1)
        def _():
            for direction in range(2):
                w_wait(direction, 0)
                w_send(direction, 2).start()
                w_sib(direction, 0).start()

        @pl.when(n == W2)
        def _():
            for direction in range(2):
                w_wait(direction, 1)
                w_sib(direction, 1).start()

        return 0

    lax.fori_loop(0, 2 * STEPS, body, 0)
    take_stats()
    attend_pair(jnp.int32(7))

    for h in range(2):
        acc[h] = acc[h] * l[h]

    def o_block(same, xt):
        mine_rows, other_rows = (0, GRP) if same else (GRP, 0)
        a = mine_rows + TOK * (4 * yh + xt)
        b = other_rows + TOK * (4 * (1 - yh) + xt)
        return jnp.concatenate(
            [acc[h, rows(r, TOK, 8), :] for r in (a, b) for h in range(2)], axis=0
        ).astype(BF16)

    def o_copy(same, dx):
        xt = (x + dx) % 4
        k = (0 if same else 4) + dx
        return remote(
            osend.at[k], orecv.at[yl * 4 + x], o_s.at[0], o_r.at[0],
            (pi if same else other, yh * 4 + xt),
        )

    order = [(False, 2), (True, 2), (False, 1), (False, 3), (True, 1), (True, 3), (False, 0)]
    for same, dx in order:
        k = (0 if same else 4) + dx
        osend[k] = o_block(same, (x + dx) % 4)
        o_copy(same, dx).start()
    osend[0] = o_block(True, x)
    pltpu.make_async_copy(osend.at[0], orecv.at[yl * 4 + x], o_r.at[0]).start()

    for direction in range(2):
        w_wait(direction, 2)
        w_sib(direction, 2).start()
    wait(wg.at[pl.ds(0, 3 * HD), :], wb_r.at[0])

    wait(orecv, o_r.at[0])
    columns = []
    for sx in range(4):
        both = orecv[sx].astype(F32) + orecv[4 + sx].astype(F32)
        for h in range(2):
            columns.append(jnp.concatenate(
                [both[h * TOK:(h + 1) * TOK], both[(2 + h) * TOK:(3 + h) * TOK]], axis=0
            ))
    attended = jnp.concatenate(columns, axis=1).astype(BF16)

    facing = (other, (1 - yh) * 4 + x)

    def b_copy(n):
        span = pl.ds(n * HALF, HALF)
        return remote(bsend.at[span, :], brecv.at[span, :], b_s.at[0], b_r.at[n], facing)

    for n in range(D // CHUNK):
        got = jnp.dot(attended, wg[:, pl.ds(n * CHUNK, CHUNK)], preferred_element_type=F32)
        bsend[pl.ds(n * HALF, HALF), :] = jnp.concatenate(
            [got[TOK:, t * HD:(t + 1) * HD] for t in range(CHUNK // HD)], axis=0
        ).astype(BF16)
        b_copy(n).start()
        afin[:, pl.ds(n * CHUNK, CHUNK)] = got[:TOK]
    for n in range(D // CHUNK):
        b_copy(n).wait_recv()
        theirs = brecv[pl.ds(n * HALF, HALF), :].astype(F32)
        theirs = jnp.concatenate([theirs[t * TOK:(t + 1) * TOK] for t in range(CHUNK // HD)], axis=1)
        span = pl.ds(n * CHUNK, CHUNK)
        mixed[:, span] = (afin[:, span] + theirs).astype(BF16)
    mixed_out.start()

    wait(kv.at[:, pl.ds(0, 7)], pass_s.at[0])
    wait(kv.at[:, z, mine, :], own_s.at[0])
    wait(qs.at[pl.ds(1, 7)], q_s.at[0])
    wait(qs, q_s.at[1])
    wait(kvs.at[pl.ds(1, 7)], f_s.at[0])
    wait(wg.at[pl.ds(0, 6 * HD), :], w_s.at[0])
    wait(stat_out, st_s.at[0])
    wait(osend.at[pl.ds(1, 7)], o_s.at[0])
    wait(bsend, b_s.at[0])
    fresh_out.wait()
    mixed_out.wait()


def hand_over(mixed_in, fresh_in, mixed_out, fresh_out):
    mixed_out[...] = mixed_in[...]
    fresh_out[...] = fresh_in[...]


def on_device(qkv, stale_kv, out_weight):
    vmem = pl.BlockSpec(memory_space=pltpu.VMEM)
    dma = pltpu.SemaphoreType.DMA
    anywhere = pl.BlockSpec(memory_space=pl.ANY)
    shapes = (
        jax.ShapeDtypeStruct((TOK, D), BF16),
        jax.ShapeDtypeStruct((2, GRP, 2 * HD), BF16),
    )
    results = pl.pallas_call(
        kernel,
        out_shape=shapes,
        in_specs=[anywhere] * 3,
        out_specs=(anywhere, anywhere),
        scratch_shapes=[
            pltpu.VMEM((3, TOK, NU * 2 * HD), BF16),
            pltpu.VMEM((4, NZ, PAIR, HD), BF16),
            pltpu.VMEM((4, PAIR, HD), BF16),
            pltpu.VMEM((2, PAIR, HD), BF16),
            pltpu.VMEM((2, NZ, PAIR, PAIR), F32),
            pltpu.VMEM((2, NZ, PAIR, PAIR), BF16),
            pltpu.VMEM((2, PAIR, HD), F32),
            pltpu.VMEM((2, PAIR, HD), F32),
            pltpu.VMEM((2, PAIR, HD), F32),
            pltpu.VMEM((2, PAIR, HD), F32),
            pltpu.VMEM((2, PAIR, HD), F32),
            pltpu.VMEM((NU, 2 * TOK, HD), BF16),
            pltpu.VMEM((NU, 4 * TOK, HD), BF16),
            pltpu.VMEM((2, NU, 2 * TOK, HD), BF16),
            pltpu.VMEM((NU, 4 * TOK, HD), BF16),
            pltpu.VMEM((8 * HD, D), BF16),
            pltpu.VMEM((8, PAIR), F32),
            pltpu.VMEM((8, PAIR), F32),
            pltpu.VMEM((8, 4 * TOK, HD), BF16),
            pltpu.VMEM((8, 4 * TOK, HD), BF16),
            pltpu.VMEM((TOK * D // HD, HD), BF16),
            pltpu.VMEM((TOK * D // HD, HD), BF16),
            pltpu.VMEM((TOK, D), F32),
            pltpu.VMEM((TOK, D), BF16),
            pltpu.VMEM((2, GRP, 2 * HD), BF16),
            dma((8,)), dma((2 * STEPS,)), dma((1,)), dma((STEPS,)), dma((1,)), dma((1,)),
            dma((2,)), dma((1,)), dma((1,)), dma((1,)), dma((1,)), dma((2, 3)), dma((1,)),
            dma((1,)), dma((1,)), dma((1,)), dma((1,)), dma((1,)), dma((D // CHUNK,)),
        ],
        compiler_params=pltpu.CompilerParams(
            collective_id=0, has_side_effects=True, vmem_limit_bytes=62 * 2**20
        ),
    )(qkv, stale_kv, out_weight)
    return pl.pallas_call(
        hand_over,
        out_shape=shapes,
        in_specs=[vmem, vmem],
        out_specs=(vmem, vmem),
    )(*results)


def solution(mesh):
    placed = (P(None, ("patch", "uly"), None), P(None, "patch", "uly"), P("uly", None))
    return jax.shard_map(
        on_device,
        mesh=mesh,
        in_specs=placed,
        out_specs=(P(("patch", "uly"), None), P(None, "patch", "uly")),
        check_vma=False,
    )
```

time: 86.8 us -> 60.1 us (0.69)
  Pallas kernels: 82.6 us -> 59.4 us
  local copies, waits for them, and re-layouts: 3.37 us -> 0 us
    pallas_call x1 -> x2, Pallas kernels: 82.6 us -> 59.4 us  [the longest x1 57.4 us: on_device(): pl.pallas_call(kernel, out_shape=shapes, in_specs=[anywhere] * 3, out_spe...]
    unnamed x2 -> x0, local copies, waits for them, and re-layouts: 3.37 us -> none
where the time goes in v2:
time: 60.1 us; the launch traced here: 60 us
  Pallas kernels  59.4 us (99%)
  between operations  0.64 us (1%)
    pallas_call x1, Pallas kernels, on_device(): pl.pallas_call(kernel, out_shape=shapes, in_specs=[anywhere] * 3, out_spe...  57.4 us
    pallas_call x1, Pallas kernels, on_device(): pl.pallas_call(hand_over, out_shape=shapes, in_specs=[vmem, vmem], out_sp...  1.93 us

profile of v2, /device:TPU:1, one launch (start us, length us, event | category | flops | bytes accessed | tf_op | source)
XLA Modules:
  0.0 60.0 jit_solution(12173751637589074510)
XLA Ops:
  0.6 57.4 %shard_map.50 = (bf16[40,3072]{1,0:T(8,128)(2,1)}, bf16[2,320,256]{2,1,0:T(8,128)(2,1)}) custom-call(bf16[3,40,2048]{2,1,0:T(8,128)(2,1)} %qkv_ref.1, bf16[2,320,256]{2,1,0:T(8,128)(2,1)} %stale_ref.1, bf16[256,3072]{1,0:T(8,128)(2,1)} %w_ref.1), custom_call_target="tpu_custom_call" | custom-call | tf_op jit(solution)/shard_map/pallas_call | solution.py:454
  58.1 1.9 %shard_map.51 = (bf16[40,3072]{1,0:T(8,128)(2,1)}, bf16[2,320,256]{2,1,0:T(8,128)(2,1)}) custom-call(bf16[40,3072]{1,0:T(8,128)(2,1)} %get-tuple-element.4.mixed_in, bf16[2,320,256]{2,1,0:T(8,128)(2,1)} %get-tuple-element.5.fresh_in), custom_call_target="tpu_custom_call" | custom-call | tf_op jit(solution)/shard_map/pallas_call | solution.py:493

commit v3 on v2

v3 whole, which is shorter than its diff:
```python
import functools

import jax
import jax.numpy as jnp
from jax import lax
from jax.experimental import pallas as pl
from jax.experimental.pallas import tpu as pltpu
from jax.sharding import PartitionSpec as P

MESH = pl.DeviceIdType.MESH
HD = 128
NZ = 8
NU = 8
TOK = 40
GRP = 320
PAIR = 640
HALF = 160
BAND = 64
OWN = 7 * PAIR
D = 3072
STEPS = 14
SCALE = HD ** -0.5 * 1.4426950408889634
NT = (((1,), (1,)), ((), ()))
F32 = jnp.float32
BF16 = jnp.bfloat16
AHEAD = 6
CHUNK = 512


def rows(offset, size, unit=16):
    return pl.ds(pl.multiple_of(offset, unit), size)


def kernel(
    qkv_ref, stale_ref, w_ref, mine_ref, their_ref, fresh_ref,
    qkv, kv, fr, q, s, p, m, top, fix, l, acc, qs, kvs, qr, kvr, wg, stat_out, stat_in,
    osend, orecv, att, bsend, afin, fresh,
    local_sem, ring_r, pass_s, sib_r, own_s, own_r, q_s, q_r, f_s, f_r,
    w_s, w_r, wb_r, wy_r, st_s, st_r, o_s, o_r, b_s, b_r,
):
    pi, u = lax.axis_index("patch"), lax.axis_index("uly")
    z, yl, c = pi // 4, (pi // 2) % 2, pi % 2
    yh, x = u // 4, u % 4

    def patch(z_, yl_, c_):
        return z_ * 4 + yl_ * 2 + c_

    sibling = (patch(z, yl, 1 - c), u)
    up = (patch((z + 1) % NZ, yl, c), u)
    down = (patch((z + 7) % NZ, yl, c), u)
    x_up = (pi, yh * 4 + (x + 1) % 4)
    x_down = (pi, yh * 4 + (x + 3) % 4)
    other = patch(z, 1 - yl, c)

    barrier = pltpu.get_barrier_semaphore()
    everyone = [sibling, up, down]
    everyone += [(pi, (u + k) % NU) for k in range(1, NU)]
    everyone += [(other, (u + k) % NU) for k in range(NU)]
    for device in everyone:
        pl.semaphore_signal(barrier, inc=1, device_id=device, device_id_type=MESH)

    def remote(src, dst, send, recv, device):
        return pltpu.make_async_remote_copy(
            src_ref=src, dst_ref=dst, send_sem=send, recv_sem=recv, device_id=device, device_id_type=MESH
        )

    mine = rows(OWN + c * GRP, GRP)
    def wait(ref, sem):
        pltpu.make_async_copy(ref, ref, sem).wait()

    qkv_in = pltpu.make_async_copy(qkv_ref, qkv, local_sem.at[7])
    locals_ = []
    for kind in range(4):
        locals_.append(pltpu.make_async_copy(
            stale_ref.at[kind // 2, :, pl.ds(kind % 2 * HD, HD)], kv.at[kind, mine, :], local_sem.at[kind]
        ))
    w_local = pltpu.make_async_copy(w_ref, wg.at[rows(x * 2 * HD, 2 * HD), :], local_sem.at[4])
    for copy in locals_:
        copy.start()
    qkv_in.start()
    w_local.start()

    for copy in locals_:
        copy.wait()
    pl.semaphore_wait(barrier, len(everyone))

    turns = ["Ka0", "Kb0", "Va0", "Ka1", "Kb1", "Vb0", "Ka2", "Kb2", "Va1", "Vb1", "Ka3", "Va2", "Vb2", "Va3"]

    def turn(n):
        phase, head, hop = turns[n // 2]
        return "KV".index(phase), 2 * int(hop) + "ab".index(head)

    def turn_of(phase, i):
        return turns.index("KV"[phase] + "ab"[i % 2] + str(i // 2))

    def place(hops, direction):
        return PAIR * {0: 7, 4: 6}.get(hops, 2 * hops - 2 + direction)

    def ring_copies(n):
        phase, i = turn(n)
        hop, head = i // 2, i % 2
        start = c * GRP + n % 2 * HALF
        for direction, device in ((0, up), (1, down)):
            kind = phase * 2 + (head if direction == 0 else 1 - head)
            yield remote(
                kv.at[kind, rows(place(hop, direction) + start, HALF), :],
                kv.at[kind, rows(place(hop + 1, direction) + start, HALF), :],
                pass_s.at[0], ring_r.at[n], device,
            )

    def sib_copies(n):
        phase, i = turn(n)
        hop, head = i // 2, i % 2
        for direction in range(2):
            kind = phase * 2 + (head if direction == 0 else 1 - head)
            slot = kv.at[kind, rows(place(hop + 1, direction) + c * GRP, GRP), :]
            yield remote(slot, slot, pass_s.at[0], sib_r.at[n // 2], sibling)

    for n in range(AHEAD):
        for copy in ring_copies(n):
            copy.start()
    own_sib = remote(kv.at[:, mine, :], kv.at[:, mine, :], own_s.at[0], own_r.at[0], sibling)
    own_sib.start()

    qkv_in.wait()
    for v in range(NU):
        parts = [
            qkv[i, :, pl.ds(v * 2 * HD + h * HD, HD)].astype(F32) for i in range(3) for h in range(2)
        ]
        qs[v] = jnp.concatenate(parts[:2], axis=0).astype(BF16)
        kvs[v] = jnp.concatenate(parts[2:], axis=0).astype(BF16)
    pltpu.make_async_copy(qs.at[u], qr.at[0, u], q_r.at[0]).start()
    pltpu.make_async_copy(kvs.at[u], kvr.at[u], f_r.at[0]).start()
    m[...] = jnp.full(m.shape, -jnp.inf, F32)
    l[...] = jnp.zeros(l.shape, F32)
    acc[...] = jnp.zeros(acc.shape, F32)

    def q_copies():
        for g, where in ((0, pi), (1, other)):
            for k in range(1 - g, NU):
                v = (u + k) % NU
                yield remote(qs.at[v], qr.at[g, u], q_s.at[g], q_r.at[0], (where, v))

    def f_copies():
        for k in range(1, NU):
            v = (u + k) % NU
            yield remote(kvs.at[v], kvr.at[u], f_s.at[0], f_r.at[0], (pi, v))

    for copy in q_copies():
        copy.start()
    for copy in f_copies():
        copy.start()

    w_order = ((("own", 0), ("own", 1), ("far", 0), ("own", 2), ("far", 1)), (("own", 2), ("own", 0), ("far", 2), ("own", 1)))

    def w_slot(origin, quarter):
        quarter = jnp.where(yl == 0, quarter, 3 - quarter)
        return wg.at[rows(origin * 2 * HD + c * HD + quarter * 32, 32), :]

    def w_piece(direction, k, at):
        whose, quarter = w_order[direction][k]
        hops = (whose == "far") + at
        return w_slot((x + 4 - hops) % 4 if direction == 0 else (x + hops) % 4, quarter)

    def w_send(direction, k):
        slot = w_piece(direction, k, 0)
        remote(slot, slot, w_s.at[0], w_r.at[direction, k], (x_up, x_down)[direction]).start()

    def w_pass(slot):
        remote(slot, slot, w_s.at[0], wb_r.at[0], sibling).start()

    def w_arrived(direction, k):
        slot = w_piece(direction, k, 1)
        wait(slot, w_r.at[direction, k])
        w_pass(slot)

    w_origins = ((x + 3) % 4, (x + 1) % 4, (x + 2) % 4)

    def w_share(k):
        slot = w_slot(w_origins[k], 0)
        remote(slot, slot, w_s.at[0], wy_r.at[k], (other, u)).start()

    def w_shared(k):
        slot = w_slot(w_origins[k], 3)
        wait(slot, wy_r.at[k])
        w_pass(slot)

    w_local.wait()
    for k in range(2):
        for direction in range(2):
            w_send(direction, k)

    def w_step(n):
        if n == 12:
            for direction in range(2):
                w_arrived(direction, 0)
                w_send(direction, 2)
                w_send(direction, 3)
            w_share(0)
        if n == 17:
            w_arrived(0, 1)
            w_arrived(1, 1)
            w_send(0, 4)
            w_share(1)
        if n == 21:
            w_arrived(0, 2)
            w_arrived(1, 2)
        if n == 24:
            w_share(2)
            w_shared(0)
        if n == 26:
            w_arrived(0, 3)
            w_arrived(1, 3)
            w_shared(1)

    def assemble_queries():
        wait(qr, q_r.at[0])
        for g in range(2):
            got = [qr[g, v].astype(F32) for v in range(NU)]
            for h in range(2):
                q[h, pl.ds(g * GRP, GRP), :] = jnp.concatenate(
                    [t[h * TOK:(h + 1) * TOK] for t in got], axis=0
                ).astype(BF16)

    fresh_out = pltpu.make_async_copy(fresh, fresh_ref, local_sem.at[5])
    mixed_out = pltpu.make_async_copy(afin, mine_ref, local_sem.at[6])

    def assemble_fresh():
        wait(kvr, f_r.at[0])
        got = [kvr[v].astype(F32) for v in range(NU)]
        for kind in range(4):
            whole = jnp.concatenate([t[kind * TOK:(kind + 1) * TOK] for t in got], axis=0).astype(BF16)
            fr[kind, rows(c * GRP, GRP), :] = whole
            fresh[kind // 2, :, pl.ds(kind % 2 * HD, HD)] = whole
        fresh_out.start()
        wait(kv.at[:, rows(OWN + (1 - c) * GRP, GRP), :], own_r.at[0])
        for kind in range(4):
            fr[kind, rows((1 - c) * GRP, GRP), :] = kv[kind, rows(OWN + (1 - c) * GRP, GRP), :]

    def note_max(h, first, scores):
        count, width = scores.shape
        for r in range(0, count, BAND):
            span = pl.ds(first + r, BAND)
            best = m[h, span, :]
            for t in range(width // HD):
                best = jnp.maximum(best, scores[r:r + BAND, t * HD:(t + 1) * HD])
            m[h, span, :] = best

    def score(h, j, width):
        scores = lax.dot_general(q[h], kv[h, rows(j * 2 * PAIR, width), :], NT, preferred_element_type=F32)
        s[h, j, :, pl.ds(0, width)] = scores
        note_max(h, 0, scores)

    def score_own(h):
        for g, keys in ((0, fr.at[h]), (1, kv.at[h, pl.ds(OWN, PAIR)])):
            span = pl.ds(g * GRP, GRP)
            scores = lax.dot_general(q[h, span, :], keys[...], NT, preferred_element_type=F32)
            s[h, 3, span, pl.ds(PAIR, PAIR)] = scores
            note_max(h, g * GRP, scores)

    def weigh(h, j, first, width):
        for r in range(0, PAIR, BAND):
            span = pl.ds(r, BAND)
            most, total = top[h, span, :], None
            for t in range(first // HD, (first + width) // HD):
                keys = pl.ds(t * HD, HD)
                weight = jnp.exp2(s[h, j, span, keys] * SCALE - most)
                total = weight if total is None else total + weight
                p[h, j, span, keys] = weight.astype(BF16)
            l[h, span, :] += total

    def attend(h, j, width):
        acc[h] += jnp.dot(
            p[h, j, :, pl.ds(0, width)], kv[2 + h, rows(j * 2 * PAIR, width), :], preferred_element_type=F32
        )

    def attend_own(h):
        for g, values in ((0, fr.at[2 + h]), (1, kv.at[2 + h, pl.ds(OWN, PAIR)])):
            span = pl.ds(g * GRP, GRP)
            acc[h, span, :] += jnp.dot(p[h, 3, span, pl.ds(PAIR, PAIR)], values[...], preferred_element_type=F32)

    def arrived(phase, i):
        wait(kv.at[0, pl.ds(0, PAIR)], sib_r.at[turn_of(phase, i)])

    def for_heads(f):
        lax.fori_loop(0, 2, lambda h, _: (f(h), 0)[1], 0)

    def row_max(h):
        return jnp.broadcast_to(jnp.max(m[h], axis=1, keepdims=True) * SCALE, (PAIR, HD))

    def first_top():
        for h in range(2):
            top[h] = row_max(h)

    def next_top():
        for h in range(2):
            old, new = top[h], row_max(h)
            top[h] = new
            fix[h] = jnp.exp2(old - new)
            l[h] = l[h] * fix[h]

    def scale_acc(h):
        acc[h] = acc[h] * fix[h]

    lane = lax.broadcasted_iota(jnp.int32, (PAIR, HD), 1)

    def stat_copy():
        return remote(stat_out, stat_in, st_s.at[0], st_r.at[0], (other, u))

    def send_stats():
        packed = jnp.zeros((PAIR, HD), F32)
        for h in range(2):
            total = jnp.broadcast_to(jnp.sum(l[h], axis=1, keepdims=True), (PAIR, HD))
            l[h] = total
            packed = jnp.where(lane == 2 * h, top[h], packed)
            packed = jnp.where(lane == 2 * h + 1, total, packed)
        stat_out[...] = packed.T[:8]
        stat_copy().start()

    def take_stats():
        stat_copy().wait_recv()
        got = jnp.concatenate([stat_in[...], jnp.zeros((HD - 8, PAIR), F32)], axis=0).T
        got = jnp.concatenate([got[GRP:], got[:GRP]], axis=0)
        for h in range(2):
            their_top, total = got[:, 2 * h:2 * h + 1], got[:, 2 * h + 1:2 * h + 2]
            mine_top, mine_total = top[h], l[h]
            most = jnp.maximum(mine_top, their_top)
            own = jnp.exp2(mine_top - most)
            l[h] = own / (mine_total * own + total * jnp.exp2(their_top - most))

    def step(n):
        wait(kv.at[0, pl.ds(0, GRP), :], ring_r.at[n])

        if n < 26 - AHEAD:
            for copy in ring_copies(n + AHEAD):
                copy.start()

        if (n == 22) or (n == 23):
            for copy in ring_copies(n + 4):
                copy.start()

        if n % 2 == 1:
            for copy in sib_copies(n):
                copy.start()

        if n == 4:
            assemble_queries()

        if (n == 4) or (n == 10) or (n == 16):
            arrived(0, (n - 4) // 3)
            arrived(0, (n - 4) // 3 + 1)

        if (n == 4) or (n == 5) or (n == 10) or (n == 11) or (n == 16) or (n == 17):
            score(n % 2, (n - 4) // 6, 2 * PAIR)

        if n == 7:
            assemble_fresh()
            for_heads(score_own)

        if n == 22:
            arrived(0, 6)
            for_heads(lambda h: score(h, 3, PAIR))

        if n == 8:
            first_top()
            for_heads(lambda h: weigh(h, 3, PAIR, PAIR))

        if n == 18:
            next_top()
            for_heads(scale_acc)

        if n == 23:
            next_top()
            for_heads(lambda h: weigh(h, 3, 0, PAIR))

        if (n == 9) or (n == 12) or ((n >= 18) and (n <= 21)):
            weigh(int(n in (12, 19, 21)), 0 if n <= 12 else 1 if n <= 19 else 2, 0, 2 * PAIR)

        if n == 23:
            send_stats()

        if n == 13:
            for_heads(attend_own)

        if (n == 14) or (n == 24) or (n == 26):
            i = {14: 0, 24: 2, 26: 4}[n]
            arrived(1, i)
            arrived(1, i + 1)

        if (n == 14) or (n == 24) or (n == 26):
            for_heads(lambda h: attend(h, i // 2, 2 * PAIR))

        w_step(n)

    for n in range(2 * STEPS):
        step(n)
    take_stats()
    for_heads(scale_acc)

    order = [(False, 2), (True, 2), (False, 1), (False, 3), (True, 1), (True, 3), (False, 0), (True, 0)]

    def hand_out(part_):
        for same, dx in order:
            xt = (x + dx) % 4
            k = (0 if same else 4) + dx
            group = GRP if same == (part_ == 1) else 0
            tokens = rows(group + TOK * (4 * ((1 - yh) if part_ == 1 else yh) + xt), TOK, 8)
            osend[part_, k] = jnp.concatenate([acc[h, tokens, :] * l[h, tokens, :] for h in range(2)], axis=0).astype(BF16)
            slot = orecv.at[part_, yl * 4 + x]
            if same and dx == 0:
                pltpu.make_async_copy(osend.at[part_, k], slot, o_r.at[part_]).start()
            else:
                remote(
                    osend.at[part_, k], slot, o_s.at[0], o_r.at[part_], (pi if same else other, yh * 4 + xt)
                ).start()

    arrived(1, 6)
    for_heads(lambda h: attend(h, 3, PAIR))
    hand_out(1)
    hand_out(0)

    w_arrived(0, 4)
    w_shared(2)
    wait(wg.at[pl.ds(0, 3 * HD), :], wb_r.at[0])

    facing = (other, (1 - yh) * 4 + x)

    def collect(part_):
        wait(orecv.at[part_], o_r.at[part_])
        columns = []
        for sx in range(4):
            both = orecv[part_, sx].astype(F32) + orecv[part_, 4 + sx].astype(F32)
            columns += [both[:TOK], both[TOK:]]
        return jnp.concatenate(columns, axis=1).astype(BF16)

    att[...] = collect(1)

    def project_theirs(n, _):
        columns = pl.ds(pl.multiple_of(n * CHUNK, CHUNK), CHUNK)
        got = jnp.dot(att[...], wg[:, columns], preferred_element_type=F32)
        span = rows(n * HALF, HALF)
        bsend[span, :] = jnp.concatenate(
            [got[:, t * HD:(t + 1) * HD] for t in range(CHUNK // HD)], axis=0
        ).astype(BF16)
        remote(bsend.at[span, :], their_ref.at[span, :], b_s.at[0], b_r.at[0], facing).start()
        return 0

    lax.fori_loop(0, D // CHUNK, project_theirs, 0)
    att[...] = collect(0)

    def project_mine(n, _):
        columns = pl.ds(pl.multiple_of(n * CHUNK, CHUNK), CHUNK)
        afin[:, columns] = jnp.dot(att[...], wg[:, columns], preferred_element_type=F32)
        return 0

    lax.fori_loop(0, D // CHUNK, project_mine, 0)
    mixed_out.start()

    wait(kv.at[:, pl.ds(0, OWN), :], pass_s.at[0])
    wait(kv.at[:, mine, :], own_s.at[0])
    wait(qs.at[pl.ds(1, 7)], q_s.at[0])
    wait(qs, q_s.at[1])
    wait(kvs.at[pl.ds(1, 7)], f_s.at[0])
    wait(wg.at[pl.ds(0, 6 * HD), :], w_s.at[0])
    wait(stat_out, st_s.at[0])
    wait(osend.at[0, pl.ds(1, 7)], o_s.at[0])
    wait(osend.at[1, pl.ds(1, 7)], o_s.at[0])
    wait(bsend, b_s.at[0])
    wait(bsend, b_r.at[0])
    fresh_out.wait()
    mixed_out.wait()


def add_up(mine_ref, their_ref, fresh_in, mixed_ref, fresh_out):
    for n in range(D // CHUNK):
        theirs = their_ref[pl.ds(n * HALF, HALF), :].astype(F32)
        theirs = jnp.concatenate([theirs[t * TOK:(t + 1) * TOK] for t in range(CHUNK // HD)], axis=1)
        span = pl.ds(n * CHUNK, CHUNK)
        mixed_ref[:, span] = (mine_ref[:, span] + theirs).astype(BF16)
    fresh_out[...] = fresh_in[...]


def on_device(qkv, stale_kv, out_weight):
    vmem = pl.BlockSpec(memory_space=pltpu.VMEM)
    dma = pltpu.SemaphoreType.DMA
    anywhere = pl.BlockSpec(memory_space=pl.ANY)
    fresh = jax.ShapeDtypeStruct((2, GRP, 2 * HD), BF16)
    results = pl.pallas_call(
        kernel,
        out_shape=(
            jax.ShapeDtypeStruct((TOK, D), F32),
            jax.ShapeDtypeStruct((TOK * D // HD, HD), BF16),
            fresh,
        ),
        in_specs=[anywhere] * 3,
        out_specs=(anywhere,) * 3,
        scratch_shapes=[
            pltpu.VMEM((3, TOK, NU * 2 * HD), BF16),
            pltpu.VMEM((4, NZ * PAIR, HD), BF16),
            pltpu.VMEM((4, PAIR, HD), BF16),
            pltpu.VMEM((2, PAIR, HD), BF16),
            pltpu.VMEM((2, NZ // 2, PAIR, 2 * PAIR), F32),
            pltpu.VMEM((2, NZ // 2, PAIR, 2 * PAIR), BF16),
            pltpu.VMEM((2, PAIR, HD), F32),
            pltpu.VMEM((2, PAIR, HD), F32),
            pltpu.VMEM((2, PAIR, HD), F32),
            pltpu.VMEM((2, PAIR, HD), F32),
            pltpu.VMEM((2, PAIR, HD), F32),
            pltpu.VMEM((NU, 2 * TOK, HD), BF16),
            pltpu.VMEM((NU, 4 * TOK, HD), BF16),
            pltpu.VMEM((2, NU, 2 * TOK, HD), BF16),
            pltpu.VMEM((NU, 4 * TOK, HD), BF16),
            pltpu.VMEM((8 * HD, D), BF16),
            pltpu.VMEM((8, PAIR), F32),
            pltpu.VMEM((8, PAIR), F32),
            pltpu.VMEM((2, 8, 2 * TOK, HD), BF16),
            pltpu.VMEM((2, 8, 2 * TOK, HD), BF16),
            pltpu.VMEM((TOK, 8 * HD), BF16),
            pltpu.VMEM((TOK * D // HD, HD), BF16),
            pltpu.VMEM((TOK, D), F32),
            pltpu.VMEM((2, GRP, 2 * HD), BF16),
            dma((8,)), dma((2 * STEPS,)), dma((1,)), dma((STEPS,)), dma((1,)), dma((1,)),
            dma((2,)), dma((1,)), dma((1,)), dma((1,)), dma((1,)), dma((2, 5)), dma((1,)), dma((3,)),
            dma((1,)), dma((1,)), dma((1,)), dma((2,)), dma((1,)), dma((1,)),
        ],
        compiler_params=pltpu.CompilerParams(
            collective_id=0, has_side_effects=True, vmem_limit_bytes=62 * 2**20
        ),
    )(qkv, stale_kv, out_weight)
    return pl.pallas_call(
        add_up,
        out_shape=(jax.ShapeDtypeStruct((TOK, D), BF16), fresh),
        in_specs=[vmem] * 3,
        out_specs=(vmem, vmem),
    )(*results)


def solution(mesh):
    placed = (P(None, ("patch", "uly"), None), P(None, "patch", "uly"), P("uly", None))
    return jax.shard_map(
        on_device,
        mesh=mesh,
        in_specs=placed,
        out_specs=(P(("patch", "uly"), None), P(None, "patch", "uly")),
        check_vma=False,
    )
```

time: 60.1 us -> 56.2 us (0.935)
  Pallas kernels: 59.4 us -> 55.4 us
    pallas_call x2, Pallas kernels: 59.4 us -> 55.4 us  [the longest x1 53.3 us: on_device(): pl.pallas_call(kernel, out_shape=(jax.ShapeDtypeStruct((TOK, D), F32), ja...]
where the time goes in v3:
time: 56.2 us; the launch traced here: 56.1 us
  Pallas kernels  55.4 us (99%)
  between operations  0.64 us (1%)
    pallas_call x1, Pallas kernels, on_device(): pl.pallas_call(kernel, out_shape=(jax.ShapeDtypeStruct((TOK, D), F32), ja...  53.3 us
    pallas_call x1, Pallas kernels, on_device(): pl.pallas_call(add_up, out_shape=(jax.ShapeDtypeStruct((TOK, D), BF16), f...  2.11 us

profile of v3, /device:TPU:1, one launch (start us, length us, event | category | flops | bytes accessed | tf_op | source)
XLA Modules:
  0.0 56.1 jit_solution(8167912164283816387)
XLA Ops:
  0.6 53.3 %shard_map.50 = (f32[40,3072]{1,0:T(8,128)}, bf16[960,128]{1,0:T(8,128)(2,1)}, bf16[2,320,256]{2,1,0:T(8,128)(2,1)}) custom-call(bf16[3,40,2048]{2,1,0:T(8,128)(2,1)} %qkv_ref.1, bf16[2,320,256]{2,1,0:T(8,128)(2,1)} %stale_ref.1, bf16[256,3072]{1,0:T(8,128)(2,1)} %w_ref.1), custom_call_target="tpu_custom_call" | custom-call | tf_op jit(solution)/shard_map/pallas_call | solution.py:488
  54.0 2.1 %shard_map.51 = (bf16[40,3072]{1,0:T(8,128)(2,1)}, bf16[2,320,256]{2,1,0:T(8,128)(2,1)}) custom-call(f32[40,3072]{1,0:T(8,128)} %get-tuple-element.5.mine_ref, bf16[960,128]{1,0:T(8,128)(2,1)} %get-tuple-element.6.their_ref, bf16[2,320,256]{2,1,0:T(8,128)(2,1)} %get-tuple-element.7.fresh_in), custom_call_target="tpu_custom_call" | custom-call | tf_op jit(solution)/shard_map/pallas_call | solution.py:530

commit v4 on v3

--- a/solution.py
+++ b/solution.py
@@ -148,10 +148,8 @@
 
     for copy in q_copies():
         copy.start()
-    for copy in f_copies():
-        copy.start()
-
-    w_order = ((("own", 0), ("own", 1), ("far", 0), ("own", 2), ("far", 1)), (("own", 2), ("own", 0), ("far", 2), ("own", 1)))
+
+    w_order = ((("own", 0), ("far", 0), ("own", 1), ("own", 2), ("far", 1)), (("own", 0), ("own", 2), ("own", 1), ("far", 2)))
 
     def w_slot(origin, quarter):
         quarter = jnp.where(yl == 0, quarter, 3 - quarter)
@@ -186,32 +184,35 @@
         w_pass(slot)
 
     w_local.wait()
-    for k in range(2):
-        for direction in range(2):
-            w_send(direction, k)
+    for direction in range(2):
+        w_send(direction, 0)
+    for copy in f_copies():
+        copy.start()
 
     def w_step(n):
-        if n == 12:
+        if n == 9:
             for direction in range(2):
                 w_arrived(direction, 0)
+                w_send(direction, 1)
                 w_send(direction, 2)
+            w_share(0)
+            w_share(1)
+        if n == 18:
+            for direction in range(2):
+                w_arrived(direction, 1)
                 w_send(direction, 3)
-            w_share(0)
-        if n == 17:
-            w_arrived(0, 1)
-            w_arrived(1, 1)
-            w_send(0, 4)
-            w_share(1)
+            w_share(2)
         if n == 21:
+            w_shared(0)
+            w_shared(1)
+        if n == 22:
             w_arrived(0, 2)
             w_arrived(1, 2)
-        if n == 24:
-            w_share(2)
-            w_shared(0)
-        if n == 26:
+            w_send(0, 4)
+        if n == 27:
             w_arrived(0, 3)
             w_arrived(1, 3)
-            w_shared(1)
+            w_shared(2)
 
     def assemble_queries():
         wait(qr, q_r.at[0])
@@ -353,7 +354,7 @@
         if (n == 4) or (n == 5) or (n == 10) or (n == 11) or (n == 16) or (n == 17):
             score(n % 2, (n - 4) // 6, 2 * PAIR)
 
-        if n == 7:
+        if n == 13:
             assemble_fresh()
             for_heads(score_own)
 
@@ -363,32 +364,37 @@
 
         if n == 8:
             first_top()
-            for_heads(lambda h: weigh(h, 3, PAIR, PAIR))
 
         if n == 18:
-            next_top()
-            for_heads(scale_acc)
+            for_heads(attend_own)
 
         if n == 23:
             next_top()
             for_heads(lambda h: weigh(h, 3, 0, PAIR))
 
-        if (n == 9) or (n == 12) or ((n >= 18) and (n <= 21)):
-            weigh(int(n in (12, 19, 21)), 0 if n <= 12 else 1 if n <= 19 else 2, 0, 2 * PAIR)
+        if (n == 8) or (n == 9) or (n == 20) or (n == 21):
+            weigh(n % 2, 0 if n <= 9 else 2, 0, 2 * PAIR)
+
+        if n == 19:
+            for_heads(lambda h: weigh(h, 1, 0, 2 * PAIR))
 
         if n == 23:
             send_stats()
 
-        if n == 13:
-            for_heads(attend_own)
-
-        if (n == 14) or (n == 24) or (n == 26):
-            i = {14: 0, 24: 2, 26: 4}[n]
+        if (n == 14) or (n == 24) or (n == 27):
+            i = {14: 0, 24: 2, 27: 4}[n]
             arrived(1, i)
             arrived(1, i + 1)
 
-        if (n == 14) or (n == 24) or (n == 26):
+        if (n == 14) or (n == 24) or (n == 27):
             for_heads(lambda h: attend(h, i // 2, 2 * PAIR))
+
+        if (n == 15) or (n == 18):
+            next_top()
+            for_heads(scale_acc)
+
+        if n == 15:
+            for_heads(lambda h: weigh(h, 3, PAIR, PAIR))
 
         w_step(n)
 
@@ -414,13 +420,23 @@
                     osend.at[part_, k], slot, o_s.at[0], o_r.at[part_], (pi if same else other, yh * 4 + xt)
                 ).start()
 
+    def attend_last(half):
+        def one(h):
+            spans = [rows(g * GRP + half * HALF, HALF) for g in range(2)]
+            weights = jnp.concatenate([p[h, 3, span, pl.ds(0, PAIR)] for span in spans], axis=0)
+            got = jnp.dot(weights, kv[2 + h, pl.ds(6 * PAIR, PAIR), :], preferred_element_type=F32)
+            for g, span in enumerate(spans):
+                acc[h, span, :] += got[g * HALF:(g + 1) * HALF]
+
+        for_heads(one)
+
     arrived(1, 6)
-    for_heads(lambda h: attend(h, 3, PAIR))
+    attend_last(1 - yh)
     hand_out(1)
+    attend_last(yh)
     hand_out(0)
 
     w_arrived(0, 4)
-    w_shared(2)
     wait(wg.at[pl.ds(0, 3 * HD), :], wb_r.at[0])
 
     facing = (other, (1 - yh) * 4 + x)

time: 56.2 us -> 55.4 us (0.986); the launches traced: 56.1 us -> 54.4 us
  Pallas kernels: 55.4 us -> 53.8 us
    pallas_call x1, Pallas kernels: 53.3 us -> 51.7 us  [on_device(): pl.pallas_call(kernel, out_shape=(jax.ShapeDtypeStruct((TOK, D), F32), ja...]
where the time goes in v4:
time: 55.4 us; the launch traced here: 54.4 us
  Pallas kernels  53.8 us (97%)
  between operations  0.64 us (1%)
    pallas_call x1, Pallas kernels, on_device(): pl.pallas_call(kernel, out_shape=(jax.ShapeDtypeStruct((TOK, D), F32), ja...  51.7 us
    pallas_call x1, Pallas kernels, on_device(): pl.pallas_call(add_up, out_shape=(jax.ShapeDtypeStruct((TOK, D), BF16), f...  2.11 us

profile of v4, /device:TPU:1, one launch (start us, length us, event | category | flops | bytes accessed | tf_op | source)
XLA Modules:
  0.0 54.4 jit_solution(8619372907067852823)
XLA Ops:
  0.6 51.7 %shard_map.50 = (f32[40,3072]{1,0:T(8,128)}, bf16[960,128]{1,0:T(8,128)(2,1)}, bf16[2,320,256]{2,1,0:T(8,128)(2,1)}) custom-call(bf16[3,40,2048]{2,1,0:T(8,128)(2,1)} %qkv_ref.1, bf16[2,320,256]{2,1,0:T(8,128)(2,1)} %stale_ref.1, bf16[256,3072]{1,0:T(8,128)(2,1)} %w_ref.1), custom_call_target="tpu_custom_call" | custom-call | tf_op jit(solution)/shard_map/pallas_call | solution.py:504
  52.3 2.1 %shard_map.51 = (bf16[40,3072]{1,0:T(8,128)(2,1)}, bf16[2,320,256]{2,1,0:T(8,128)(2,1)}) custom-call(f32[40,3072]{1,0:T(8,128)} %get-tuple-element.5.mine_ref, bf16[960,128]{1,0:T(8,128)(2,1)} %get-tuple-element.6.their_ref, bf16[2,320,256]{2,1,0:T(8,128)(2,1)} %get-tuple-element.7.fresh_in), custom_call_target="tpu_custom_call" | custom-call | tf_op jit(solution)/shard_map/pallas_call | solution.py:546

commit v5 on v4

--- a/solution.py
+++ b/solution.py
@@ -195,12 +195,13 @@
                 w_arrived(direction, 0)
                 w_send(direction, 1)
                 w_send(direction, 2)
+            w_send(0, 3)
             w_share(0)
             w_share(1)
         if n == 18:
             for direction in range(2):
                 w_arrived(direction, 1)
-                w_send(direction, 3)
+            w_send(1, 3)
             w_share(2)
         if n == 21:
             w_shared(0)

time: 55.4 us -> 55.4 us (level)
  no operation moved by 1% of the time
where the time goes in v5:
time: 55.4 us; the launch traced here: 54.4 us
  Pallas kernels  53.8 us (97%)
  between operations  0.64 us (1%)
    pallas_call x1, Pallas kernels, on_device(): pl.pallas_call(kernel, out_shape=(jax.ShapeDtypeStruct((TOK, D), F32), ja...  51.7 us
    pallas_call x1, Pallas kernels, on_device(): pl.pallas_call(add_up, out_shape=(jax.ShapeDtypeStruct((TOK, D), BF16), f...  2.11 us

profile of v5, /device:TPU:1, one launch (start us, length us, event | category | flops | bytes accessed | tf_op | source)
XLA Modules:
  0.0 54.4 jit_solution(15611345576183119252)
XLA Ops:
  0.6 51.7 %shard_map.50 = (f32[40,3072]{1,0:T(8,128)}, bf16[960,128]{1,0:T(8,128)(2,1)}, bf16[2,320,256]{2,1,0:T(8,128)(2,1)}) custom-call(bf16[3,40,2048]{2,1,0:T(8,128)(2,1)} %qkv_ref.1, bf16[2,320,256]{2,1,0:T(8,128)(2,1)} %stale_ref.1, bf16[256,3072]{1,0:T(8,128)(2,1)} %w_ref.1), custom_call_target="tpu_custom_call" | custom-call | tf_op jit(solution)/shard_map/pallas_call | solution.py:505
  52.3 2.1 %shard_map.51 = (bf16[40,3072]{1,0:T(8,128)(2,1)}, bf16[2,320,256]{2,1,0:T(8,128)(2,1)}) custom-call(f32[40,3072]{1,0:T(8,128)} %get-tuple-element.5.mine_ref, bf16[960,128]{1,0:T(8,128)(2,1)} %get-tuple-element.6.their_ref, bf16[2,320,256]{2,1,0:T(8,128)(2,1)} %get-tuple-element.7.fresh_in), custom_call_target="tpu_custom_call" | custom-call | tf_op jit(solution)/shard_map/pallas_call | solution.py:547
